TPU v7x, 32 devices: a whole 2x2x4 slice. The times are simulated.
32 devices in a mesh: rec: 8 (over y, x, core), chan: 4 (over z).
Axes of the slice: x: 2, y: 2, z: 4, core: 2. Of those that a mesh axis runs over, the one named last changes fastest.
Arguments:
- signal: bfloat16 [4, 32, 307200], P(None, 'chan', 'rec'), may hold values from -6 to 6
- montage: int32 [4, 4, 8], P(None, 'chan'), may hold values from 0 to 7, each once within a row
- channels: int32 [4], replicated, may hold values from 19 to 32
- lengths: int32 [4], replicated, may hold values from 769 to 1536
- boundary: int32 [4, 1536], P(None, 'rec'), may hold values 0 or 1
- conv_in: bfloat16 [8, 4, 5, 200, 128], P('rec', 'chan'), may hold values from -0.1875 to 0.1875
- conv_hid: bfloat16 [8, 4, 2, 5, 128, 128], P('rec', 'chan'), may hold values from -0.25 to 0.25
- mix_weight: bfloat16 [8, 4, 128, 512], P(None, 'chan'), may hold values from -0.09375 to 0.09375
- norm_gain: float32 [512], replicated, may hold values from 0.1 to 1.9
- emit_weight: float32 [512, 5], replicated, may hold values from -1 to 1
- trans_within: float32 [5, 5], replicated, may hold values from -3 to 3
- trans_between: float32 [5, 5], replicated, may hold values from -2 to 102
- initial: float32 [5], replicated, may hold values from -6 to 6
Outputs:
- filtered: float32 [4, 5, 1536], P(None, None, 'rec')
- log_rate: float32 [4], replicated
All inputs are finite; a program needn't handle non-finite values. No bound on the sum of `boundary` on one device may be relied on, other than what follows from the above.
Results may differ from a plain program's by a relative error of at most 0.011.
Values may be sent and summed in bfloat16 or wider, within the bound.
A program may use at most 128 MiB of HBM per device.

v0:
```python
import functools

import jax
import jax.numpy as jnp
from jax import lax
from jax.experimental import pallas as pl
from jax.experimental.pallas import tpu as pltpu
from jax.sharding import PartitionSpec as P

SAMP = 200
EMB = 128
STATES = 5


EPSILON = 1e-05
NEGATIVE = -1e30


LANES = 128


def lse_list(terms):
    peak = terms[0]
    for term in terms[1:]:
        peak = jnp.maximum(peak, term)
    total = jnp.exp(terms[0] - peak)
    for term in terms[1:]:
        total = total + jnp.exp(term - peak)
    return peak + jnp.log(total)


def peak_of(matrix):
    peak = matrix[0]
    for entry in matrix[1:]:
        peak = jnp.maximum(peak, entry)
    return peak


def crf_kernel(
    field_ref, length_ref, within_ref, between_ref, initial_ref, filtered_ref, total_ref
):
    steps, recordings = field_ref.shape[1], field_ref.shape[2]
    shape = (recordings, LANES)
    lane = lax.broadcasted_iota(jnp.int32, shape, 1)
    length = length_ref[...]
    states = range(STATES)
    identity = [jnp.full(shape, 0.0 if i == s else NEGATIVE) for i in states for s in states]

    def transition(step):
        cross = field_ref[STATES, step] > 0.5
        return [
            jnp.where(cross, between_ref[i, s], within_ref[i, s]) for i in states for s in states
        ]

    def grow(step, matrix):
        moves = transition(step)
        valid = lane * steps + step < length
        grown = []
        for i in states:
            for s in states:
                moved = lse_list([matrix[i * STATES + k] + moves[k * STATES + s] for k in states])
                grown.append(
                    jnp.where(valid, moved + field_ref[s, step], matrix[i * STATES + s])
                )
        return tuple(grown)

    moves = transition(0)
    valid = lane * steps < length
    matrix = tuple(
        jnp.where(valid, moves[i * STATES + s] + field_ref[s, 0], identity[i * STATES + s])
        for i in states
        for s in states
    )
    matrix = lax.fori_loop(1, steps, grow, matrix)
    offset = peak_of(matrix)
    matrix = [entry - offset for entry in matrix]
    distance = 1
    while distance < LANES:
        inside = lane >= distance
        before = [
            jnp.where(inside, pltpu.roll(entry, distance, 1), unit)
            for entry, unit in zip(matrix, identity)
        ]
        offset = offset + jnp.where(inside, pltpu.roll(offset, distance, 1), 0.0)
        product = [
            lse_list([before[i * STATES + k] + matrix[k * STATES + s] for k in states])
            for i in states
            for s in states
        ]
        peak = peak_of(product)
        matrix = [entry - peak for entry in product]
        offset = offset + peak
        distance *= 2
    prior = [jnp.full(shape, initial_ref[s]) for s in states]
    level = lse_list(prior)
    prior = [entry - level for entry in prior]
    reached = [lse_list([prior[i] + matrix[i * STATES + s] for i in states]) for s in states]
    level = lse_list(reached)
    total_ref[...] = level + offset
    start = tuple(
        jnp.where(lane >= 1, pltpu.roll(entry - level, 1, 1), unit)
        for entry, unit in zip(reached, prior)
    )

    def advance(step, vector):
        moves = transition(step)
        valid = lane * steps + step < length
        moved = [
            lse_list([vector[i] + moves[i * STATES + s] for i in states]) + field_ref[s, step]
            for s in states
        ]
        height = lse_list(moved)
        vector = tuple(
            jnp.where(valid, entry - height, old) for entry, old in zip(moved, vector)
        )
        for s in states:
            filtered_ref[step, s] = vector[s]
        return vector

    lax.fori_loop(0, steps, advance, start)


def crf(field, lengths, within, between, initial):
    steps, recordings = field.shape[1], field.shape[2]
    vmem = pl.BlockSpec(memory_space=pltpu.VMEM)
    smem = pl.BlockSpec(memory_space=pltpu.SMEM)
    return pl.pallas_call(
        crf_kernel,
        out_shape=(
            jax.ShapeDtypeStruct((steps, STATES, recordings, LANES), jnp.float32),
            jax.ShapeDtypeStruct((recordings, LANES), jnp.float32),
        ),
        in_specs=[vmem, vmem, smem, smem, smem],
        out_specs=(vmem, vmem),
    )(
        field,
        jnp.broadcast_to(lengths[:, None], (recordings, LANES)),
        within,
        between,
        initial,
    )


MESH = pl.DeviceIdType.MESH
VMEM_LIMIT = 52 * 1024 * 1024
HALO = 8
DEPTH = 208


def vmem_spec():
    return pl.BlockSpec(memory_space=pltpu.VMEM)


def cut_kernel(pick_ref, live_ref, signal_ref, left_ref, right_ref, rows_ref, low_ref, high_ref):
    lines = signal_ref.shape[0]
    types, total = rows_ref.shape[0], rows_ref.shape[1]
    recordings = pick_ref.shape[0]
    length = total // recordings
    patches = length - 2 * HALO
    reach = left_ref.shape[1]
    live = live_ref[...] > 0

    def put(chunk, offset, row):
        piece = chunk[:, offset : offset + SAMP]
        low_ref[pl.ds(row * lines, lines), :] = piece[:, :128]
        high_ref[pl.ds(row * lines, lines), :] = jnp.concatenate(
            [piece[:, 128:], jnp.zeros((lines, 256 - SAMP), jnp.float32)], axis=1
        )

    def kept(block):
        return jnp.where(live, block.astype(jnp.float32), 0.0)

    blank = jnp.zeros((2 * lines, 128), jnp.float32)
    for part in (low_ref, high_ref):
        part[pl.ds(0, 2 * lines), :] = blank
        part[pl.ds((length - 2) * lines, 2 * lines), :] = blank
    left = kept(left_ref[...])
    right = kept(right_ref[...])
    for q in range(6):
        put(left, reach - (6 - q) * SAMP, 2 + q)
        put(right, q * SAMP, HALO + patches + q)
    period = 16

    def cut(step, carry):
        start = pl.multiple_of(step * (period * SAMP), 128)
        block = kept(signal_ref[:, pl.ds(start, period * SAMP)])
        for q in range(period):
            put(block, q * SAMP, HALO + step * period + q)
        return carry

    lax.fori_loop(0, patches // period, cut, 0)

    def pick(item, carry):
        kind, recording = item // recordings, item % recordings
        line = recording * types + pick_ref[recording, kind]
        place = pl.ds(pl.multiple_of(recording * length, 16), length)
        low = low_ref[pl.ds(line, length, stride=lines), :]
        high = high_ref[pl.ds(line, length, stride=lines), :]
        rows_ref[kind, place, 0:128] = low.astype(jnp.bfloat16)
        rows_ref[kind, place, 128:DEPTH] = high[:, : DEPTH - 128].astype(jnp.bfloat16)
        return carry

    lax.fori_loop(0, types * recordings, pick, 0)


def encode_kernel(
    recordings, rows_ref, taps_ref, mix_ref, out_ref, held, wide, encoded, send, relay, recv, local
):
    types, total = rows_ref.shape[0], rows_ref.shape[1]
    length = total // recordings
    patches = length - 2 * HALO
    half = types // 2
    me = lax.axis_index("rec")
    pair, parity = me // 2, me % 2
    partner = 2 * pair + (1 - parity)

    barrier = pltpu.get_barrier_semaphore()
    for d in range(1, half):
        peer = 2 * ((pair + half - d) % half) + parity
        pl.semaphore_signal(barrier, inc=1, device_id={"rec": peer}, device_id_type=MESH)
    pl.semaphore_signal(barrier, inc=1, device_id={"rec": partner}, device_id_type=MESH)
    pl.semaphore_wait(barrier, half)

    sends = []
    own = pltpu.make_async_remote_copy(
        src_ref=taps_ref,
        dst_ref=held.at[me],
        send_sem=send.at[0],
        recv_sem=recv.at[me],
        device_id={"rec": partner},
        device_id_type=MESH,
    )
    own.start()
    sends.append(own)
    for d in range(1, half):
        peer = 2 * ((pair + half - d) % half) + parity
        copy = pltpu.make_async_remote_copy(
            src_ref=taps_ref,
            dst_ref=held.at[me],
            send_sem=send.at[d],
            recv_sem=recv.at[me],
            device_id={"rec": peer},
            device_id_type=MESH,
        )
        copy.start()
        sends.append(copy)
    keep = pltpu.make_async_copy(taps_ref, held.at[me], local)
    keep.start()
    edge = jnp.zeros((8, wide.shape[2]), jnp.float32)
    for slot in range(2):
        wide[slot, 0:8, :] = edge
        wide[slot, 8 + length : 16 + length, :] = edge
    position = lax.broadcasted_iota(jnp.int32, (length, EMB), 0) - HALO + me * patches
    inside = jnp.logical_and(position >= 0, position < types * patches)
    keep.wait()

    def conv(values, weights, slot):
        wide[slot, 8 : 8 + length, :] = jnp.dot(
            values, weights, preferred_element_type=jnp.float32
        )
        taps = weights.shape[1] // EMB
        first = 8 - taps // 2
        result = wide[slot, first : first + length, 0:EMB]
        for k in range(1, taps):
            result = result + wide[slot, first + k : first + k + length, k * EMB : (k + 1) * EMB]
        return jax.nn.gelu(result)

    depth_count = (taps_ref.shape[0] - DEPTH) // EMB

    def encode(source):
        def one(recording, slot):
            start = pl.multiple_of(recording * length, 16)
            patch_rows = rows_ref[source, pl.ds(start, length), :]
            current = conv(patch_rows, held[source, 0:DEPTH, :], slot)
            current = jnp.where(inside, current, 0.0).astype(jnp.bfloat16)
            for layer in range(depth_count):
                base = DEPTH + layer * EMB
                update = conv(current, held[source, base : base + EMB, :], slot)
                current = current.astype(jnp.float32) + update
                current = jnp.where(inside, current, 0.0).astype(jnp.bfloat16)
            encoded[
                pl.ds(pl.multiple_of(recording * patches, 16), patches),
                pl.ds(pl.multiple_of(source * EMB, EMB), EMB),
            ] = current[HALO : HALO + patches]

        def two(step, carry):
            one(2 * step, 0)
            one(2 * step + 1, 1)
            return carry

        lax.fori_loop(0, recordings // 2, two, 0)

    def arrival(slot):
        return pltpu.make_async_remote_copy(
            src_ref=taps_ref,
            dst_ref=held.at[slot],
            send_sem=send.at[0],
            recv_sem=recv.at[slot],
            device_id={"rec": partner},
            device_id_type=MESH,
        )

    for h in range(half):
        near = 2 * ((pair + h) % half) + parity
        far = 2 * ((pair + h) % half) + (1 - parity)
        if h > 0:
            arrival(near).wait_recv()
            forward = pltpu.make_async_remote_copy(
                src_ref=held.at[near],
                dst_ref=held.at[near],
                send_sem=relay.at[h],
                recv_sem=recv.at[near],
                device_id={"rec": partner},
                device_id_type=MESH,
            )
            forward.start()
            sends.append(forward)
        encode(near)
        arrival(far).wait_recv()
        encode(far)

    block = 2 * EMB

    def mix(step, carry):
        rows = pl.ds(pl.multiple_of(step * block, block), block)
        out_ref[rows, :] = jnp.dot(
            encoded[rows, :], mix_ref[...], preferred_element_type=jnp.float32
        ).astype(jnp.bfloat16)
        return carry

    lax.fori_loop(0, recordings * patches // block, mix, 0)
    for copy in sends:
        copy.wait_send()


def tail_kernel(
    part_ref, gain_ref, head_ref, extra_ref, out_ref,
    landed, column, spread, send1, recv1, send2, recv2, send3, recv3,
):
    columns, rows = part_ref.shape[0], part_ref.shape[1]
    groups = out_ref.shape[0]
    mine, me = lax.axis_index("chan"), lax.axis_index("rec")
    barrier = pltpu.get_barrier_semaphore()
    for d in range(1, columns):
        pl.semaphore_signal(
            barrier, inc=1, device_id={"chan": (mine + d) % columns}, device_id_type=MESH
        )
    for d in range(1, groups):
        pl.semaphore_signal(
            barrier, inc=1, device_id={"rec": (me + d) % groups}, device_id_type=MESH
        )
    pl.semaphore_wait(barrier, columns + groups - 2)

    def scatter(d):
        peer = (mine + d) % columns
        return pltpu.make_async_remote_copy(
            src_ref=part_ref.at[peer],
            dst_ref=landed.at[d],
            send_sem=send1.at[d],
            recv_sem=recv1.at[d],
            device_id={"chan": peer},
            device_id_type=MESH,
        )

    def along_chan(d):
        return pltpu.make_async_remote_copy(
            src_ref=column.at[mine],
            dst_ref=column.at[mine],
            send_sem=send2.at[d],
            recv_sem=recv2.at[d],
            device_id={"chan": (mine + d) % columns},
            device_id_type=MESH,
        )

    def along_rec(d):
        return pltpu.make_async_remote_copy(
            src_ref=column,
            dst_ref=spread.at[me],
            send_sem=send3.at[d],
            recv_sem=recv3.at[d],
            device_id={"rec": (me + d) % groups},
            device_id_type=MESH,
        )

    for d in range(1, columns):
        scatter(d).start()
    summed = part_ref[mine].astype(jnp.float32)
    for d in range(1, columns):
        scatter(d).wait()
        summed = summed + landed[d].astype(jnp.float32)
    average = jnp.mean(summed, axis=-1, keepdims=True)
    centred = summed - average
    variance = jnp.mean(centred * centred, axis=-1, keepdims=True)
    activated = jax.nn.gelu(centred * lax.rsqrt(variance + EPSILON) * gain_ref[...])
    emission = lax.dot_general(
        head_ref[...],
        activated,
        (((1,), (1,)), ((), ())),
        precision=lax.Precision.HIGHEST,
        preferred_element_type=jnp.float32,
    )
    column[mine] = jnp.zeros(column.shape[1:], jnp.float32)
    column[mine, :, 0:rows] = emission + extra_ref[...]
    for d in range(1, columns):
        along_chan(d).start()
    for d in range(1, columns):
        along_chan(d).wait()
    for d in range(1, groups):
        along_rec(d).start()
    out_ref[me] = column[...]
    for d in range(1, groups):
        along_rec(d).wait()
        source = (me + groups - d) % groups
        out_ref[source] = spread[source]


def local(
    signal,
    montage,
    channels,
    lengths,
    boundary,
    conv_in,
    conv_hid,
    mix_weight,
    norm_gain,
    emit_weight,
    trans_within,
    trans_between,
    initial,
):
    groups = lax.axis_size("rec")
    columns = lax.axis_size("chan")
    chan_index = lax.axis_index("chan")
    rec_index = lax.axis_index("rec")
    recordings, _, samples = signal.shape
    patches = samples // SAMP
    features = mix_weight.shape[-1]
    reach = -(-6 * SAMP // 128) * 128
    lines = recordings * groups
    flat = signal.reshape(lines, samples)
    ahead = [(i, i + 1) for i in range(groups - 1)]
    back = [(i + 1, i) for i in range(groups - 1)]
    left = lax.ppermute(flat[:, samples - reach :], "rec", ahead)
    right = lax.ppermute(flat[:, :reach], "rec", back)
    slot_ids = chan_index * groups + jnp.arange(groups, dtype=jnp.int32)
    live = (slot_ids[None, :] < channels[:, None]).astype(jnp.int32).reshape(lines, 1)
    places = jnp.arange(groups, dtype=jnp.int32)
    matches = montage[:, 0, :, None] == places[None, None, :]
    inverse = jnp.sum(jnp.where(matches, places[None, :, None], 0), axis=1)
    length = patches + 2 * HALO
    patch_rows = pl.pallas_call(
        cut_kernel,
        out_shape=jax.ShapeDtypeStruct((groups, recordings * length, DEPTH), jnp.bfloat16),
        in_specs=[pl.BlockSpec(memory_space=pltpu.SMEM)] + [vmem_spec()] * 4,
        out_specs=vmem_spec(),
        scratch_shapes=[pltpu.VMEM((length * lines, 128), jnp.float32)] * 2,
        compiler_params=pltpu.CompilerParams(vmem_limit_bytes=VMEM_LIMIT),
    )(inverse, live, flat, left, right)

    first = jnp.transpose(conv_in[0, 0], (1, 0, 2)).reshape(SAMP, -1)
    hidden = jnp.transpose(conv_hid[0, 0], (0, 2, 1, 3)).reshape(-1, first.shape[1])
    blank = jnp.zeros((DEPTH - SAMP, first.shape[1]), jnp.bfloat16)
    taps = jnp.concatenate([first, blank, hidden], axis=0)
    partial = pl.pallas_call(
        functools.partial(encode_kernel, recordings),
        out_shape=jax.ShapeDtypeStruct((recordings * patches, features), jnp.bfloat16),
        in_specs=[vmem_spec()] * 3,
        out_specs=vmem_spec(),
        scratch_shapes=[
            pltpu.VMEM((groups,) + taps.shape, jnp.bfloat16),
            pltpu.VMEM((2, length + 16, taps.shape[1]), jnp.float32),
            pltpu.VMEM((recordings * patches, groups * EMB), jnp.bfloat16),
            pltpu.SemaphoreType.DMA((groups // 2,)),
            pltpu.SemaphoreType.DMA((groups // 2,)),
            pltpu.SemaphoreType.DMA((groups,)),
            pltpu.SemaphoreType.DMA,
        ],
        compiler_params=pltpu.CompilerParams(
            collective_id=0, has_side_effects=True, vmem_limit_bytes=VMEM_LIMIT
        ),
    )(patch_rows, taps, mix_weight[:, 0].reshape(groups * EMB, features))

    rows = recordings * patches // columns
    padded = -(-rows // 128) * 128
    cross = lax.dynamic_slice_in_dim(boundary.reshape(-1), chan_index * rows, rows)
    cross = (cross == 1).astype(jnp.float32)
    extra = jnp.pad(cross[None], ((STATES, 2), (0, 0)))
    head = jnp.pad(emit_weight.T, ((0, 8 - STATES), (0, 0)))
    field = pl.pallas_call(
        tail_kernel,
        out_shape=jax.ShapeDtypeStruct((groups, columns, 8, padded), jnp.float32),
        in_specs=[vmem_spec()] * 4,
        out_specs=vmem_spec(),
        scratch_shapes=[
            pltpu.VMEM((columns, rows, features), jnp.bfloat16),
            pltpu.VMEM((columns, 8, padded), jnp.float32),
            pltpu.VMEM((groups, columns, 8, padded), jnp.float32),
        ]
        + [pltpu.SemaphoreType.DMA((count,)) for count in (columns, columns) * 2 + (groups, groups)],
        compiler_params=pltpu.CompilerParams(
            collective_id=1, has_side_effects=True, vmem_limit_bytes=VMEM_LIMIT
        ),
    )(partial.reshape(columns, rows, features), norm_gain[None], head, extra)

    wide = LANES // groups
    steps = patches // wide
    field = field[:, :, : STATES + 1, :rows]
    field = jnp.transpose(field, (0, 2, 1, 3)).reshape(
        groups, STATES + 1, recordings, wide, steps
    )
    field = jnp.transpose(field, (1, 4, 2, 0, 3)).reshape(STATES + 1, steps, recordings, LANES)
    history, total = crf(field, lengths, trans_within, trans_between, initial)
    own = lax.dynamic_slice_in_dim(history, rec_index * wide, wide, axis=3)
    filtered = jnp.transpose(own, (2, 1, 3, 0)).reshape(recordings, STATES, patches)
    return filtered, total[:, LANES - 1] / lengths.astype(jnp.float32)


def solution(mesh):
    placed = (
        P(None, "chan", "rec"),
        P(None, "chan", None),
        P(),
        P(),
        P(None, "rec"),
        P("rec", "chan", None, None, None),
        P("rec", "chan", None, None, None, None),
        P(None, "chan", None, None),
        P(),
        P(),
        P(),
        P(),
        P(),
    )
    return jax.shard_map(
        local, mesh=mesh, in_specs=placed, out_specs=(P(None, None, "rec"), P()), check_vma=False
    )
```

profile of v0, /device:TPU:0, one launch (start us, length us, event | category | flops | bytes accessed | tf_op | source)
XLA Modules:
  0.0 110.9 jit_solution(1028693437955557411)
XLA Ops:
  0.6 1.0 fusion
  1.6 2.4 %collective-permute-start = (bf16[32,1280]{1,0:T(8,128)(2,1)S(1)}, bf16[32,1280]{1,0:T(8,128)(2,1)S(1)}, u32[]{:S(2)}, u32[]{:S(2)}) collective-permute-start(bf16[32,1280]{1,0:T(8,128)(2,1)S(1)} %get-tuple-element.7), channel_id=1, source_target_pairs={{0,4},{4,8},{8,12},{12,16},{16,20},{20,24},{24,28},{1,5},{5,9},{9,... | collective-permute-start | bytes 245768 | tf_op jit(solution)/shard_map/ppermute | solution.py:444
  4.0 1.3 %collective-permute-start.1 = (bf16[32,1280]{1,0:T(8,128)(2,1)S(1)}, bf16[32,1280]{1,0:T(8,128)(2,1)S(1)}, u32[]{:S(2)}, u32[]{:S(2)}) collective-permute-start(bf16[32,1280]{1,0:T(8,128)(2,1)S(1)} %get-tuple-element.6), channel_id=1, source_target_pairs={{4,0},{8,4},{12,8},{16,12},{20,16},{24,20},{28,24},{5,1},{9,5},{13... | collective-permute-start | bytes 245768 | tf_op jit(solution)/shard_map/ppermute | solution.py:445
  5.3 0.8 select_reduce_fusion.pick_ref
  6.1 0.7 compare_convert_fusion
  6.8 0.1 reshape.72.live_ref
  6.9 1.2 %copy.35 = bf16[2,128,5,128]{3,2,1,0:T(8,128)(2,1)S(1)} copy(bf16[2,128,5,128]{3,1,2,0:T(8,128)(2,1)} %bitcast.42) | data formatting | bytes 655360 | tf_op jit(solution)/shard_map/reshape | solution.py:462
  8.1 0.0 copy-start.3
  8.1 0.0 copy-start.2
  8.1 0.1 copy.40
  8.2 0.2 copy.28
  8.4 0.2 copy.30
  8.6 0.2 copy-done.3
  8.8 0.1 reshape.67
  8.9 0.1 dynamic-slice_compare_fusion
  9.0 0.1 pad.14.clone
  9.1 0.2 pad_maximum_fusion.taps_ref
  9.3 0.0 collective-permute-done.1.right_ref
  9.3 13.0 %shard_map.140.rows_ref = bf16[8,832,208]{2,1,0:T(8,128)(2,1)} custom-call(s32[4,8]{1,0:T(4,128)S(1)} %select_reduce_fusion.pick_ref, s32[32,1]{1,0:T(8,128)S(1)} %reshape.72.live_ref, bf16[32,38400]{1,0:T(8,128)(2,1)} %bitcast.37, bf16[32,1280]{1,0:T(8,128)(2,1)S(1)} %collective-permute-done.left_ref, bf16[32,1280]{1,0:T(8,128)(2,1)S(1)} %collective-permute-done.1.right_ref), custom_call_target="tpu_custom_call" | custom-call | tf_op jit(solution)/shard_map/pallas_call | solution.py:452
  22.2 42.1 %shard_map.141 = bf16[768,512]{1,0:T(8,128)(2,1)S(1)} custom-call(bf16[8,832,208]{2,1,0:T(8,128)(2,1)} %shard_map.140.rows_ref, bf16[464,640]{1,0:T(8,128)(2,1)S(1)} %pad_maximum_fusion.taps_ref, bf16[1024,512]{1,0:T(8,128)(2,1)} %bitcast.41), custom_call_target="tpu_custom_call" | custom-call | tf_op jit(solution)/shard_map/pallas_call | solution.py:465
  64.3 34.8 %shard_map.142 = f32[8,4,8,256]{3,2,1,0:T(8,128)S(1)} custom-call(bf16[4,192,512]{2,1,0:T(8,128)(2,1)S(1)} %bitcast.33, f32[1,512]{1,0:T(1,128)S(1)} %bitcast.34, f32[8,512]{1,0:T(8,128)S(1)} %pad.10.head_ref, f32[8,192]{1,0:T(8,128)S(1)} %pad_convert_fusion.extra_ref), custom_call_target="tpu_custom_call" | custom-call | tf_op jit(solution)/shard_map/pallas_call | solution.py:490
  99.1 0.1 copy.32
  99.2 0.9 reshape.68
  100.1 0.0 copy-start.4
  100.2 1.1 %copy.36.field_ref = f32[6,12,4,128]{3,2,1,0:T(4,128)} copy(f32[6,12,4,128]{1,3,2,0:T(8,128)S(1)} %bitcast.35) | data formatting | bytes 294912 | tf_op jit(solution)/shard_map/reshape | solution.py:512
  101.3 0.6 broadcast_in_dim.37.length_ref
  101.9 5.6 %shard_map.143 = (f32[12,5,4,128]{3,2,1,0:T(4,128)}, f32[4,128]{1,0:T(4,128)}) custom-call(f32[6,12,4,128]{3,2,1,0:T(4,128)} %copy.36.field_ref, s32[4,128]{1,0:T(4,128)} %broadcast_in_dim.37.length_ref, f32[5,5]{1,0:T(8,128)} %within_ref.1, f32[5,5]{1,0:T(8,128)} %between_ref.1, f32[5]{0:T(128)} %initial_ref.1), custom_call_target="tpu_custom_call" | custom-call | tf_op jit(solution)/shard_map/pallas_call | solution.py:127
  107.6 1.0 dynamic-slice_bitcast_fusion
  108.6 0.2 copy.34
  108.8 0.7 reshape.70
  109.5 0.9 slice_reduce_fusion
  110.4 0.5 convert_divide_fusion
  (13 shorter events, 0.1 us)
Async XLA Ops:
  0.6 7.6 %copy-start.1 = (bf16[1,1,5,200,128]{4,3,2,1,0:T(8,128)(2,1)S(1)}, bf16[1,1,5,200,128]{4,3,2,1,0:T(8,128)(2,1)}, u32[]{:S(2)}) copy-start(bf16[1,1,5,200,128]{4,3,2,1,0:T(8,128)(2,1)} %param.18) | copy-start | bytes 768004
  1.6 7.6 %collective-permute-start = (bf16[32,1280]{1,0:T(8,128)(2,1)S(1)}, bf16[32,1280]{1,0:T(8,128)(2,1)S(1)}, u32[]{:S(2)}, u32[]{:S(2)}) collective-permute-start(bf16[32,1280]{1,0:T(8,128)(2,1)S(1)} %get-tuple-element.7), channel_id=1, source_target_pairs={{0,4},{4,8},{8,12},{12,16},{16,20},{20,24},{24,28},{1,5},{5,9},{9,... | collective-permute-start | bytes 245768 | tf_op jit(solution)/shard_map/ppermute | solution.py:444
  4.0 5.3 %collective-permute-start.1 = (bf16[32,1280]{1,0:T(8,128)(2,1)S(1)}, bf16[32,1280]{1,0:T(8,128)(2,1)S(1)}, u32[]{:S(2)}, u32[]{:S(2)}) collective-permute-start(bf16[32,1280]{1,0:T(8,128)(2,1)S(1)} %get-tuple-element.6), channel_id=1, source_target_pairs={{4,0},{8,4},{12,8},{16,12},{20,16},{24,20},{28,24},{5,1},{9,5},{13... | collective-permute-start | bytes 245768 | tf_op jit(solution)/shard_map/ppermute | solution.py:445
  8.1 0.7 copy-start.3
  8.1 0.9 copy-start.2
  22.2 42.1 %copy-start = (f32[512]{0:T(512)S(1)}, f32[512]{0:T(512)}, u32[]{:S(2)}) copy-start(f32[512]{0:T(512)} %param.21) | copy-start | bytes 6148
  100.1 1.1 %copy-start.4 = (s32[4]{0:T(128)S(1)}, s32[4]{0:T(128)}, u32[]{:S(2)}) copy-start(s32[4]{0:T(128)} %param.16) | copy-start | bytes 52
where the time goes:
time: 111 us
  Pallas kernels  95.4 us (86%)
  local copies, waits for them, and re-layouts  8.75 us (8%)
  starting transfers between devices  3.65 us (3%)
  other arithmetic  2.28 us (2%)
    pallas_call x1, Pallas kernels, local(): pl.pallas_call(functools.partial(encode_kernel, recordings), out_shape=ja...  42.1 us
    pallas_call x1, Pallas kernels, local(): pl.pallas_call(tail_kernel, out_shape=jax.ShapeDtypeStruct((groups, colum...  34.8 us
    pallas_call x1, Pallas kernels, local(): pl.pallas_call(cut_kernel, out_shape=jax.ShapeDtypeStruct((groups, record...  13 us
    pallas_call x1, Pallas kernels, crf(): pl.pallas_call(crf_kernel, out_shape=(jax.ShapeDtypeStruct((steps, STATES...  5.62 us
    ppermute x1, starting transfers between devices, local(): left = lax.ppermute(flat[:, samples - reach:], 'rec', ahead)  2.36 us
  transfers between devices with their start and end apart: 2, of which 0 were waited for; matrix products, arithmetic and copies ran while one was open for 3% of the time, Pallas kernels for 0%

commit v1 on v0

--- a/solution.py
+++ b/solution.py
@@ -1,5 +1,3 @@
-import functools
-
 import jax
 import jax.numpy as jnp
 from jax import lax
@@ -151,7 +149,7 @@
     return pl.BlockSpec(memory_space=pltpu.VMEM)
 
 
-def cut_kernel(pick_ref, live_ref, signal_ref, left_ref, right_ref, rows_ref, low_ref, high_ref):
+def cut_rows(pick_ref, live_ref, signal_ref, left_ref, right_ref, rows_ref, low_ref, high_ref):
     lines = signal_ref.shape[0]
     types, total = rows_ref.shape[0], rows_ref.shape[1]
     recordings = pick_ref.shape[0]
@@ -204,8 +202,10 @@
 
 
 def encode_kernel(
-    recordings, rows_ref, taps_ref, mix_ref, out_ref, held, wide, encoded, send, relay, recv, local
+    pick_ref, live_ref, signal_ref, left_ref, right_ref, taps_ref, mix_ref, out_ref,
+    rows_ref, low_ref, high_ref, held, wide, encoded, send, recv, second, local,
 ):
+    recordings = pick_ref.shape[0]
     types, total = rows_ref.shape[0], rows_ref.shape[1]
     length = total // recordings
     patches = length - 2 * HALO
@@ -214,36 +214,38 @@
     pair, parity = me // 2, me % 2
     partner = 2 * pair + (1 - parity)
 
+    square = half == 4
+    if square:
+        side, over = pair + 1 - 2 * (pair % 2), (pair + 2) % 4
+        order, peers = [pair, side, over, 3 - pair], [side, over]
+    else:
+        order = [(pair + h) % half for h in range(half)]
+        peers = [(pair + half - d) % half for d in range(1, half)]
+    near = [2 * base + parity for base in order]
+    far = [2 * base + (1 - parity) for base in order]
+    targets = [partner] + [2 * peer + parity for peer in peers]
+
     barrier = pltpu.get_barrier_semaphore()
-    for d in range(1, half):
-        peer = 2 * ((pair + half - d) % half) + parity
-        pl.semaphore_signal(barrier, inc=1, device_id={"rec": peer}, device_id_type=MESH)
-    pl.semaphore_signal(barrier, inc=1, device_id={"rec": partner}, device_id_type=MESH)
-    pl.semaphore_wait(barrier, half)
+    for target in targets:
+        pl.semaphore_signal(barrier, inc=1, device_id={"rec": target}, device_id_type=MESH)
+    pl.semaphore_wait(barrier, len(targets))
 
     sends = []
-    own = pltpu.make_async_remote_copy(
-        src_ref=taps_ref,
-        dst_ref=held.at[me],
-        send_sem=send.at[0],
-        recv_sem=recv.at[me],
-        device_id={"rec": partner},
-        device_id_type=MESH,
-    )
-    own.start()
-    sends.append(own)
-    for d in range(1, half):
-        peer = 2 * ((pair + half - d) % half) + parity
+
+    def push(source, destination, target, semaphore):
         copy = pltpu.make_async_remote_copy(
-            src_ref=taps_ref,
-            dst_ref=held.at[me],
-            send_sem=send.at[d],
-            recv_sem=recv.at[me],
-            device_id={"rec": peer},
+            src_ref=source,
+            dst_ref=destination,
+            send_sem=send.at[len(sends)],
+            recv_sem=semaphore,
+            device_id={"rec": target},
             device_id_type=MESH,
         )
         copy.start()
         sends.append(copy)
+
+    for target in targets[1:] + targets[:1]:
+        push(taps_ref, held.at[me], target, recv.at[me])
     keep = pltpu.make_async_copy(taps_ref, held.at[me], local)
     keep.start()
     edge = jnp.zeros((8, wide.shape[2]), jnp.float32)
@@ -252,6 +254,9 @@
         wide[slot, 8 + length : 16 + length, :] = edge
     position = lax.broadcasted_iota(jnp.int32, (length, EMB), 0) - HALO + me * patches
     inside = jnp.logical_and(position >= 0, position < types * patches)
+    cut_rows(
+        pick_ref, live_ref, signal_ref, left_ref, right_ref, rows_ref, low_ref, high_ref
+    )
     keep.wait()
 
     def conv(values, weights, slot):
@@ -290,34 +295,61 @@
 
         lax.fori_loop(0, recordings // 2, two, 0)
 
-    def arrival(slot):
-        return pltpu.make_async_remote_copy(
-            src_ref=taps_ref,
-            dst_ref=held.at[slot],
+    def await_block(block, semaphore):
+        pltpu.make_async_remote_copy(
+            src_ref=block,
+            dst_ref=block,
             send_sem=send.at[0],
-            recv_sem=recv.at[slot],
+            recv_sem=semaphore,
             device_id={"rec": partner},
             device_id_type=MESH,
-        )
-
-    for h in range(half):
-        near = 2 * ((pair + h) % half) + parity
-        far = 2 * ((pair + h) % half) + (1 - parity)
-        if h > 0:
-            arrival(near).wait_recv()
-            forward = pltpu.make_async_remote_copy(
-                src_ref=held.at[near],
-                dst_ref=held.at[near],
-                send_sem=relay.at[h],
-                recv_sem=recv.at[near],
-                device_id={"rec": partner},
-                device_id_type=MESH,
-            )
-            forward.start()
-            sends.append(forward)
-        encode(near)
-        arrival(far).wait_recv()
-        encode(far)
+        ).wait_recv()
+
+    def arrived(slot):
+        await_block(held.at[slot], recv.at[slot])
+
+    def forward(slot):
+        push(held.at[slot], held.at[slot], partner, recv.at[slot])
+
+    if square:
+        split = taps_ref.shape[0] // 32 * 16
+        rest = taps_ref.shape[0] - split
+
+        def upper(slot):
+            return held.at[slot, pl.ds(0, split)]
+
+        def lower(slot):
+            return held.at[slot, pl.ds(split, rest)]
+
+        encode(near[0])
+        arrived(near[1])
+        push(upper(near[1]), upper(near[1]), targets[2], recv.at[near[1]])
+        arrived(near[2])
+        push(lower(near[2]), lower(near[2]), targets[1], second)
+        forward(near[1])
+        forward(near[2])
+        arrived(far[0])
+        encode(far[0])
+        encode(near[1])
+        await_block(upper(near[3]), recv.at[near[3]])
+        await_block(lower(near[3]), second)
+        forward(near[3])
+        arrived(far[1])
+        encode(far[1])
+        encode(near[2])
+        arrived(far[2])
+        encode(far[2])
+        encode(near[3])
+        arrived(far[3])
+        encode(far[3])
+    else:
+        for h in range(half):
+            if h > 0:
+                arrived(near[h])
+                forward(near[h])
+            encode(near[h])
+            arrived(far[h])
+            encode(far[h])
 
     block = 2 * EMB
 
@@ -449,37 +481,31 @@
     matches = montage[:, 0, :, None] == places[None, None, :]
     inverse = jnp.sum(jnp.where(matches, places[None, :, None], 0), axis=1)
     length = patches + 2 * HALO
-    patch_rows = pl.pallas_call(
-        cut_kernel,
-        out_shape=jax.ShapeDtypeStruct((groups, recordings * length, DEPTH), jnp.bfloat16),
-        in_specs=[pl.BlockSpec(memory_space=pltpu.SMEM)] + [vmem_spec()] * 4,
-        out_specs=vmem_spec(),
-        scratch_shapes=[pltpu.VMEM((length * lines, 128), jnp.float32)] * 2,
-        compiler_params=pltpu.CompilerParams(vmem_limit_bytes=VMEM_LIMIT),
-    )(inverse, live, flat, left, right)
-
     first = jnp.transpose(conv_in[0, 0], (1, 0, 2)).reshape(SAMP, -1)
     hidden = jnp.transpose(conv_hid[0, 0], (0, 2, 1, 3)).reshape(-1, first.shape[1])
     blank = jnp.zeros((DEPTH - SAMP, first.shape[1]), jnp.bfloat16)
     taps = jnp.concatenate([first, blank, hidden], axis=0)
     partial = pl.pallas_call(
-        functools.partial(encode_kernel, recordings),
+        encode_kernel,
         out_shape=jax.ShapeDtypeStruct((recordings * patches, features), jnp.bfloat16),
-        in_specs=[vmem_spec()] * 3,
+        in_specs=[pl.BlockSpec(memory_space=pltpu.SMEM)] + [vmem_spec()] * 6,
         out_specs=vmem_spec(),
         scratch_shapes=[
+            pltpu.VMEM((groups, recordings * length, DEPTH), jnp.bfloat16),
+            pltpu.VMEM((length * lines, 128), jnp.float32),
+            pltpu.VMEM((length * lines, 128), jnp.float32),
             pltpu.VMEM((groups,) + taps.shape, jnp.bfloat16),
             pltpu.VMEM((2, length + 16, taps.shape[1]), jnp.float32),
             pltpu.VMEM((recordings * patches, groups * EMB), jnp.bfloat16),
-            pltpu.SemaphoreType.DMA((groups // 2,)),
-            pltpu.SemaphoreType.DMA((groups // 2,)),
+            pltpu.SemaphoreType.DMA((groups + 2,)),
             pltpu.SemaphoreType.DMA((groups,)),
+            pltpu.SemaphoreType.DMA,
             pltpu.SemaphoreType.DMA,
         ],
         compiler_params=pltpu.CompilerParams(
             collective_id=0, has_side_effects=True, vmem_limit_bytes=VMEM_LIMIT
         ),
-    )(patch_rows, taps, mix_weight[:, 0].reshape(groups * EMB, features))
+    )(inverse, live, flat, left, right, taps, mix_weight[:, 0].reshape(groups * EMB, features))
 
     rows = recordings * patches // columns
     padded = -(-rows // 128) * 128

time: 111 us -> 95.9 us (0.86)
  Pallas kernels: 95.4 us -> 80.1 us
    pallas_call x2 -> x1, Pallas kernels: 55 us -> 43.9 us  [local(): pl.pallas_call(encode_kernel, out_shape=jax.ShapeDtypeStruct((recordings...]
    pallas_call x1, Pallas kernels: 34.8 us -> 30.5 us  [local(): pl.pallas_call(tail_kernel, out_shape=jax.ShapeDtypeStruct((groups, colum...]
  transfers between devices with their start and end apart: 2 -> 2, of which waited for: 0 -> 0; matrix products, arithmetic and copies ran while one was open for 3% -> 4% of each run, Pallas kernels for 0% -> 0%
where the time goes in v1:
time: 95.9 us; the launch traced here: 95.6 us
  Pallas kernels  80.1 us (84%)
  local copies, waits for them, and re-layouts  9.43 us (10%)
  starting transfers between devices  3.65 us (4%)
  other arithmetic  1.59 us (2%)
    pallas_call x1, Pallas kernels, local(): pl.pallas_call(encode_kernel, out_shape=jax.ShapeDtypeStruct((recordings...  43.9 us
    pallas_call x1, Pallas kernels, local(): pl.pallas_call(tail_kernel, out_shape=jax.ShapeDtypeStruct((groups, colum...  30.5 us
    pallas_call x1, Pallas kernels, crf(): pl.pallas_call(crf_kernel, out_shape=(jax.ShapeDtypeStruct((steps, STATES...  5.62 us
    ppermute x1, starting transfers between devices, local(): left = lax.ppermute(flat[:, samples - reach:], 'rec', ahead)  2.36 us
  transfers between devices with their start and end apart: 2, of which 0 were waited for; matrix products, arithmetic and copies ran while one was open for 4% of the time, Pallas kernels for 0%

profile of v1, /device:TPU:0, one launch (start us, length us, event | category | flops | bytes accessed | tf_op | source)
XLA Modules:
  0.0 95.6 jit_solution(2308121307704759422)
XLA Ops:
  0.6 1.0 %fusion = (bf16[32,1280]{1,0:T(8,128)(2,1)S(1)}, bf16[32,1280]{1,0:T(8,128)(2,1)S(1)}) fusion(bf16[32,38400]{1,0:T(8,128)(2,1)} %bitcast.36), kind=kLoop, calls=%fused_computation.12 | loop fusion | bytes 327680 | tf_op jit(solution)/shard_map/slice | solution.py:477
  1.6 2.4 %collective-permute-start = (bf16[32,1280]{1,0:T(8,128)(2,1)S(1)}, bf16[32,1280]{1,0:T(8,128)(2,1)S(1)}, u32[]{:S(2)}, u32[]{:S(2)}) collective-permute-start(bf16[32,1280]{1,0:T(8,128)(2,1)S(1)} %get-tuple-element.7), channel_id=1, source_target_pairs={{0,4},{4,8},{8,12},{12,16},{16,20},{20,24},{24,28},{1,5},{5,9},{9,... | collective-permute-start | bytes 245768 | tf_op jit(solution)/shard_map/ppermute | solution.py:476
  4.0 1.3 %collective-permute-start.1 = (bf16[32,1280]{1,0:T(8,128)(2,1)S(1)}, bf16[32,1280]{1,0:T(8,128)(2,1)S(1)}, u32[]{:S(2)}, u32[]{:S(2)}) collective-permute-start(bf16[32,1280]{1,0:T(8,128)(2,1)S(1)} %get-tuple-element.6), channel_id=1, source_target_pairs={{4,0},{8,4},{12,8},{16,12},{20,16},{24,20},{28,24},{5,1},{9,5},{13... | collective-permute-start | bytes 245768 | tf_op jit(solution)/shard_map/ppermute | solution.py:477
  5.3 0.8 reshape.67
  6.1 0.1 dynamic-slice_compare_fusion
  6.2 0.7 compare_convert_fusion
  6.9 0.1 reshape.72.live_ref
  7.0 1.2 %copy.35 = bf16[2,128,5,128]{3,2,1,0:T(8,128)(2,1)S(1)} copy(bf16[2,128,5,128]{3,1,2,0:T(8,128)(2,1)} %bitcast.42) | data formatting | bytes 655360 | tf_op jit(solution)/shard_map/reshape | solution.py:485
  8.2 0.0 copy-start.3
  8.2 0.0 copy-start.2
  8.2 0.1 copy.40
  8.3 0.2 copy.27
  8.5 0.2 copy.29
  8.6 0.2 copy-done.3
  8.9 0.1 select_reduce_fusion.pick_ref
  9.0 0.1 pad.14.clone
  9.0 0.2 pad_maximum_fusion.taps_ref
  9.2 0.0 collective-permute-done.left_ref
  9.2 0.0 collective-permute-done.1.right_ref
  9.3 43.9 %shard_map.140 = bf16[768,512]{1,0:T(8,128)(2,1)S(1)} custom-call(s32[4,8]{1,0:T(4,128)S(1)} %select_reduce_fusion.pick_ref, s32[32,1]{1,0:T(8,128)S(1)} %reshape.72.live_ref, bf16[32,38400]{1,0:T(8,128)(2,1)} %bitcast.37, bf16[32,1280]{1,0:T(8,128)(2,1)S(1)} %collective-permute-done.left_ref, bf16[32,1280]{1,0:T(8,128)(2,1)S(1)} %collective-permute-done.1.right_ref, ...), custom_call_target="tpu_custom_call" | custom-call | tf_op jit(solution)/shard_map/pallas_call | solution.py:488
  53.2 30.5 %shard_map.141 = f32[8,4,8,256]{3,2,1,0:T(8,128)S(1)} custom-call(bf16[4,192,512]{2,1,0:T(8,128)(2,1)S(1)} %bitcast.33, f32[1,512]{1,0:T(1,128)S(1)} %bitcast.34, f32[8,512]{1,0:T(8,128)S(1)} %pad.10.head_ref, f32[8,192]{1,0:T(8,128)S(1)} %pad_convert_fusion.extra_ref), custom_call_target="tpu_custom_call" | custom-call | tf_op jit(solution)/shard_map/pallas_call | solution.py:516
  83.8 0.1 copy.32
  83.9 0.9 reshape.68
  84.8 0.0 copy-start.4
  84.8 1.1 %copy.36.field_ref = f32[6,12,4,128]{3,2,1,0:T(4,128)} copy(f32[6,12,4,128]{1,3,2,0:T(8,128)S(1)} %bitcast.35) | data formatting | bytes 294912 | tf_op jit(solution)/shard_map/reshape | solution.py:538
  85.9 0.6 broadcast_in_dim.37.length_ref
  86.6 5.6 %shard_map.142 = (f32[12,5,4,128]{3,2,1,0:T(4,128)}, f32[4,128]{1,0:T(4,128)}) custom-call(f32[6,12,4,128]{3,2,1,0:T(4,128)} %copy.36.field_ref, s32[4,128]{1,0:T(4,128)} %broadcast_in_dim.37.length_ref, f32[5,5]{1,0:T(8,128)} %within_ref.1, f32[5,5]{1,0:T(8,128)} %between_ref.1, f32[5]{0:T(128)} %initial_ref.1), custom_call_target="tpu_custom_call" | custom-call | tf_op jit(solution)/shard_map/pallas_call | solution.py:125
  92.2 1.0 %dynamic-slice_bitcast_fusion = f32[4,5,16,12]{2,0,1,3:T(4,128)S(1)} fusion(f32[12,5,4,128]{3,2,1,0:T(4,128)} %get-tuple-element.4, s32[]{:T(128)S(6)} %select_n.12), kind=kLoop, calls=%fused_computation.3 | loop fusion | bytes 30724 | tf_op jit(solution)/shard_map/transpose | solution.py:541
  93.2 0.2 copy.34
  93.4 0.7 reshape.70
  94.2 0.9 slice_reduce_fusion
  95.0 0.5 convert_divide_fusion
  (12 shorter events, 0.1 us)
Async XLA Ops:
  0.6 7.6 %copy-start.1 = (bf16[1,1,5,200,128]{4,3,2,1,0:T(8,128)(2,1)S(1)}, bf16[1,1,5,200,128]{4,3,2,1,0:T(8,128)(2,1)}, u32[]{:S(2)}) copy-start(bf16[1,1,5,200,128]{4,3,2,1,0:T(8,128)(2,1)} %param.18) | copy-start | bytes 768004
  1.6 7.6 %collective-permute-start = (bf16[32,1280]{1,0:T(8,128)(2,1)S(1)}, bf16[32,1280]{1,0:T(8,128)(2,1)S(1)}, u32[]{:S(2)}, u32[]{:S(2)}) collective-permute-start(bf16[32,1280]{1,0:T(8,128)(2,1)S(1)} %get-tuple-element.7), channel_id=1, source_target_pairs={{0,4},{4,8},{8,12},{12,16},{16,20},{20,24},{24,28},{1,5},{5,9},{9,... | collective-permute-start | bytes 245768 | tf_op jit(solution)/shard_map/ppermute | solution.py:476
  4.0 5.3 %collective-permute-start.1 = (bf16[32,1280]{1,0:T(8,128)(2,1)S(1)}, bf16[32,1280]{1,0:T(8,128)(2,1)S(1)}, u32[]{:S(2)}, u32[]{:S(2)}) collective-permute-start(bf16[32,1280]{1,0:T(8,128)(2,1)S(1)} %get-tuple-element.6), channel_id=1, source_target_pairs={{4,0},{8,4},{12,8},{16,12},{20,16},{24,20},{28,24},{5,1},{9,5},{13... | collective-permute-start | bytes 245768 | tf_op jit(solution)/shard_map/ppermute | solution.py:477
  8.2 0.7 copy-start.3
  8.2 0.8 copy-start.2
  9.3 44.0 %copy-start = (f32[512]{0:T(512)S(1)}, f32[512]{0:T(512)}, u32[]{:S(2)}) copy-start(f32[512]{0:T(512)} %param.21) | copy-start | bytes 6148
  84.8 1.1 %copy-start.4 = (s32[4]{0:T(128)S(1)}, s32[4]{0:T(128)}, u32[]{:S(2)}) copy-start(s32[4]{0:T(128)} %param.16) | copy-start | bytes 52
